TPU v7x, 32 devices: a whole 2x2x4 slice. The times are simulated.
32 devices in a mesh: dp: 2 (over y), tm: 4 (over x, core), height: 4 (over z).
Axes of the slice: x: 2, y: 2, z: 4, core: 2. Of those that a mesh axis runs over, the one named last changes fastest.
Arguments:
- low_frames: bfloat16 [2, 16, 16, 32, 256], P('dp', 'tm', 'height'), may hold values from -6 to 6
- spatial_weight: bfloat16 [3, 3, 256, 256], replicated, may hold values from -0.125 to 0.125
- temporal_weight: bfloat16 [3, 256, 256], replicated, may hold values from -0.21875 to 0.21875
- cotangent: bfloat16 [2, 16, 32, 64, 256], P('dp', 'tm', 'height'), may hold values from -6 to 6
Outputs:
- section_out: bfloat16 [2, 16, 32, 64, 256], P('dp', 'tm', 'height')
- input_grad: bfloat16 [2, 16, 16, 32, 256], P('dp', 'tm', 'height')
- spatial_grad: float32 [3, 3, 256, 256], replicated
- temporal_grad: float32 [3, 256, 256], replicated
All inputs are finite; a program needn't handle non-finite values.
Results may differ from a plain program's by a relative error of at most 0.0033.
Values may be sent and summed in bfloat16 or wider, within the bound.
No kernel may reach another device: no remote copies, remote signals or barrier semaphores. Data moves between devices by JAX's collectives and lax.ppermute only.
A program may use at most 64 MiB of HBM per device.

v0:
```python
import jax
import jax.numpy as jnp
from jax import lax
from jax.sharding import PartitionSpec as P


def extended(block, sides, width):
    for axis, dim in sides:
        count = lax.axis_size(axis)
        forward = [(i, i + 1) for i in range(count - 1)]
        backward = [(target, source) for source, target in forward]
        low = lax.ppermute(
            lax.slice_in_dim(block, block.shape[dim] - width, None, axis=dim), axis, forward
        )
        high = lax.ppermute(lax.slice_in_dim(block, 0, width, axis=dim), axis, backward)
        block = jnp.concatenate([low, block, high], axis=dim)
    return block


def shifted(block, axis, distance):
    devices = range(lax.axis_size(axis))
    route = [(i - distance, i) for i in devices if i - distance in devices]
    return lax.ppermute(block, axis, route)


def spatial_apply(padded, weights, rows, cols):
    chan = weights.shape[-1]
    total = jnp.zeros((padded.shape[0] * rows * cols, chan), jnp.float32)
    for i in range(3):
        for j in range(3):
            piece = padded[:, i : i + rows, j : j + cols, :].reshape(-1, chan)
            total = total + jnp.dot(piece, weights[i, j], preferred_element_type=jnp.float32)
    return total


def on_device(low_frames, spatial_weight, temporal_weight, cotangent):
    low = low_frames[0]
    grad_out = cotangent[0]
    frames, rows_low, cols_low, chan = low.shape
    rows = 2 * rows_low
    cols = 2 * cols_low
    low_ext = extended(low, (("height", 1),), 1)
    upsampled = jnp.repeat(jnp.repeat(low_ext, 2, axis=1), 2, axis=2)[:, 1:-1]
    padded = jnp.pad(upsampled, ((0, 0), (0, 0), (1, 1), (0, 0)))
    pre = spatial_apply(padded, spatial_weight, rows, cols)
    act = jax.nn.silu(pre).astype(jnp.bfloat16).reshape(frames, rows, cols, chan)
    earlier = shifted(act[frames - 2 :], "tm", 1)
    act_ext = jnp.concatenate([earlier, act], 0)
    mixed = padded[:, 1:-1, 1:-1, :].reshape(-1, chan).astype(jnp.float32)
    for k in range(3):
        mixed = mixed + jnp.dot(
            act_ext[2 - k : 2 - k + frames].reshape(-1, chan),
            temporal_weight[k],
            preferred_element_type=jnp.float32,
        )
    section_out = mixed.astype(jnp.bfloat16).reshape(1, frames, rows, cols, chan)
    later = shifted(grad_out[:2], "tm", -1)
    grad_ext = jnp.concatenate([grad_out, later], 0)
    grad_flat = grad_out.reshape(-1, chan)
    act_grad = jnp.zeros((frames * rows * cols, chan), jnp.float32)
    tgrads = []
    for k in range(3):
        act_grad = act_grad + jnp.dot(
            grad_ext[k : k + frames].reshape(-1, chan),
            temporal_weight[k].T,
            preferred_element_type=jnp.float32,
        )
        tgrads.append(
            lax.dot_general(
                act_ext[2 - k : 2 - k + frames].reshape(-1, chan),
                grad_flat,
                (((0,), (0,)), ((), ())),
                preferred_element_type=jnp.float32,
            )
        )
    temporal_grad = jnp.stack(tgrads)
    sig = jax.nn.sigmoid(pre)
    pre_grad = (act_grad * (sig * (1.0 + pre * (1.0 - sig)))).astype(jnp.bfloat16)
    sgrads = []
    for i in range(3):
        for j in range(3):
            piece = padded[:, i : i + rows, j : j + cols, :].reshape(-1, chan)
            sgrads.append(
                lax.dot_general(
                    piece, pre_grad, (((0,), (0,)), ((), ())), preferred_element_type=jnp.float32
                )
            )
    spatial_grad = jnp.stack(sgrads).reshape(3, 3, chan, chan)
    grad_rows = extended(pre_grad.reshape(frames, rows, cols, chan), (("height", 1),), 1)
    grad_pad = jnp.pad(grad_rows, ((0, 0), (0, 0), (1, 1), (0, 0)))
    total = grad_flat.astype(jnp.float32)
    for i in range(3):
        for j in range(3):
            piece = grad_pad[:, 2 - i : 2 - i + rows, 2 - j : 2 - j + cols, :].reshape(-1, chan)
            total = total + jnp.dot(
                piece, spatial_weight[i, j].T, preferred_element_type=jnp.float32
            )
    input_grad = (
        total.reshape(frames, rows_low, 2, cols_low, 2, chan).sum(axis=(2, 4)).astype(jnp.bfloat16)
    )
    spatial_grad, temporal_grad = lax.psum((spatial_grad, temporal_grad), ("dp", "tm", "height"))
    return (section_out, input_grad[None], spatial_grad, temporal_grad)


def solution(mesh):
    in_specs = (P("dp", "tm", "height", None, None), P(), P(), P("dp", "tm", "height", None, None))
    out_specs = (P("dp", "tm", "height", None, None), P("dp", "tm", "height", None, None), P(), P())
    return jax.shard_map(
        on_device, mesh=mesh, in_specs=in_specs, out_specs=out_specs, check_vma=False
    )
```

profile of v0, /device:TPU:0, one launch (start us, length us, event | category | flops | bytes accessed | tf_op | source)
XLA Modules:
  0.0 207.5 jit_solution(18385429145028293199)
XLA Ops:
  7.2 0.9 fusion.77
  8.1 4.9 %collective-permute-start = (bf16[4,1,32,256]{3,2,1,0:T(8,128)(2,1)S(1)}, bf16[4,1,32,256]{3,2,1,0:T(8,128)(2,1)S(1)}, u32[]{:S(2)}, u32[]{:S(2)}) collective-permute-start(bf16[4,1,32,256]{3,2,1,0:T(8,128)(2,1)S(1)} %get-tuple-element.29), channel_id=1, source_target_pairs={{0,1},{1,2},{2,3},{4,5},{5,6},{6,7},{8,9},{9,10},{10,11},{12,13},{... | collective-permute-start | bytes 196616 | tf_op jit(solution)/shard_map/ppermute | solution.py:12
  13.1 1.4 collective-permute-start.1
  14.5 1.9 slice_bitcast_fusion
  16.4 1.3 collective-permute-start.3
  17.7 3.0 %fusion.26 = f32[2048,256]{1,0:T(8,128)} fusion(bf16[2048,256]{1,0:T(8,128)(2,1)} %bitcast.190, bf16[3,256,256]{2,1,0:T(8,128)(2,1)} %param.6), kind=kOutput, calls=%fused_computation.80 | convolution fusion | flops 268435456 | bytes 3276800 | tf_op jit(solution)/shard_map/dot_general | solution.py:63
  20.8 1.4 broadcast_in_dim.8
  22.2 0.6 reshape.117
  23.4 4.2 %pad_slice_fusion.4 = (bf16[4,8,64,256]{3,2,1,0:T(8,128)(2,1)S(1)}, bf16[4,8,64,256]{3,2,1,0:T(8,128)(2,1)S(1)}, bf16[4,8,64,256]{3,2,1,0:T(8,128)(2,1)S(1)}, bf...) fusion(bf16[4,10,64,256]{3,2,1,0:T(8,128)(2,1)S(1)} %slice.207), kind=kLoop, calls=%fused_computation.66 | loop fusion | bytes 7602176 | tf_op jit(solution)/shard_map/slice | solution.py:31
  31.1 0.7 multiply_convert_fusion
  31.9 3.2 %collective-permute-start.2 = (bf16[2,8,64,256]{3,2,1,0:T(8,128)(2,1)S(1)}, bf16[2,8,64,256]{3,2,1,0:T(8,128)(2,1)S(1)}, u32[]{:S(2)}, u32[]{:S(2)}) collective-permute-start(bf16[2,8,64,256]{3,2,1,0:T(8,128)(2,1)S(1)} %bitcast.235), channel_id=1, source_target_pairs={{0,4},{4,8},{8,12},{1,5},{5,9},{9,13},{2,6},{6,10},{10,14},{3,7},{... | collective-permute-start | bytes 1572872 | tf_op jit(solution)/shard_map/ppermute | solution.py:23
  35.1 0.5 convolution_bitcast_fusion.2
  36.1 1.4 pad_maximum_fusion.2
  37.9 0.5 convolution_add_fusion.8
  38.4 1.1 fusion.4
  39.4 0.5 fusion.19
  39.9 0.7 fusion.76
  40.6 4.5 %collective-permute-start.4 = (bf16[4,1,64,256]{3,2,1,0:T(8,128)(2,1)}, bf16[4,1,64,256]{3,2,1,0:T(8,128)(2,1)S(1)}, u32[]{:S(2)}, u32[]{:S(2)}) collective-permute-start(bf16[4,1,64,256]{3,2,1,0:T(8,128)(2,1)} %get-tuple-element.27), channel_id=1, source_target_pairs={{0,1},{1,2},{2,3},{4,5},{5,6},{6,7},{8,9},{9,10},{10,11},{12,13},{... | collective-permute-start | bytes 393224 | tf_op jit(solution)/shard_map/ppermute | solution.py:12
  45.2 1.5 collective-permute-start.5
  46.6 0.5 fusion.18
  47.1 0.5 fusion.17
  47.6 0.5 fusion.16
  48.1 0.5 fusion.15
  48.6 0.5 fusion.14
  49.1 0.5 fusion.13
  49.6 0.5 fusion.12
  50.1 0.5 fusion.11
  50.8 0.5 convolution_bitcast_fusion.1
  51.3 0.7 copy-done.3
  52.5 0.5 convolution_bitcast_fusion
  52.9 1.4 fusion.5
  54.4 0.9 pad_maximum_fusion.4
  55.3 0.8 fusion.10
  56.1 1.1 fusion.75
  57.2 0.5 fusion.42
  57.7 0.5 convolution_add_fusion.6
  58.3 0.5 fusion.2
  58.8 0.5 convolution_add_fusion.4
  59.3 0.5 fusion.29
  59.8 0.5 convolution_add_fusion.3
  60.2 0.5 convolution_add_fusion.2
  60.7 0.5 convolution_add_fusion.1
  61.2 0.5 fusion.1
  61.7 2.5 %reshape.142 = f32[4,4,2,32,2,256]{5,4,3,2,1,0:T(2,128)} reshape(f32[2048,256]{1,0:T(8,128)S(1)} %fusion.1) | data formatting | bytes 4194304 | tf_op jit(solution)/shard_map/reshape | solution.py:99
  64.2 4.0 %reduce_sum.9 = bf16[4,4,32,256]{3,2,1,0:T(8,128)(2,1)} reduce(f32[4,4,2,32,2,256]{5,4,3,2,1,0:T(2,128)} %reshape.142, f32[]{:T(128)} %constant.8.clone.1), dimensions={2,4}, to_apply=%region_0.1 | reduce | flops 393216 | bytes 2359300 | tf_op jit(solution)/shard_map/reduce_sum | solution.py:99
  68.2 128.3 %all-reduce.5.cloned.1.call-done = (f32[3,3,256,256]{3,2,1,0:T(8,128)}, f32[3,256,256]{2,1,0:T(8,128)}) async-done(((f32[3,3,256,256]{3,2,1,0:T(8,128)}, f32[3,256,256]{2,1,0:T(8,128)}), (f32[3,3,256,256]{3,2,1,0:T(8,128)}, f32[3,256,256]{2,1,0:T(8,128)})) %all-reduce.5.cloned.1.call-update) | async-done | bytes 3145744 | tf_op jit(solution)/shard_map/psum | solution.py:101
  196.5 3.3 %copy.18 = f32[3,3,256,256]{3,2,1,0:T(8,128)} copy(f32[3,3,256,256]{3,2,1,0:T(8,128)} %get-tuple-element.35) | data formatting | bytes 4718592
  199.8 0.9 copy.19
  (38 shorter events, 5.8 us)
Async XLA Ops:
  7.2 189.3 %all-reduce.5.cloned.1.call-start = ((), (), s32[]{:S(2)}) async-start(), calls=%async_computation | async-start | bytes 6291456 | tf_op jit(solution)/shard_map/psum | solution.py:101
  8.1 12.6 %collective-permute-start = (bf16[4,1,32,256]{3,2,1,0:T(8,128)(2,1)S(1)}, bf16[4,1,32,256]{3,2,1,0:T(8,128)(2,1)S(1)}, u32[]{:S(2)}, u32[]{:S(2)}) collective-permute-start(bf16[4,1,32,256]{3,2,1,0:T(8,128)(2,1)S(1)} %get-tuple-element.29), channel_id=1, source_target_pairs={{0,1},{1,2},{2,3},{4,5},{5,6},{6,7},{8,9},{9,10},{10,11},{12,13},{... | collective-permute-start | bytes 196616 | tf_op jit(solution)/shard_map/ppermute | solution.py:12
  13.0 7.6 %copy-start.6 = (bf16[1,4,4,32,256]{4,3,2,1,0:T(8,128)(2,1)S(1)}, bf16[1,4,4,32,256]{4,3,2,1,0:T(8,128)(2,1)}, u32[]{:S(2)}) copy-start(bf16[1,4,4,32,256]{4,3,2,1,0:T(8,128)(2,1)} %param.4) | copy-start | bytes 786436
  13.1 7.6 %collective-permute-start.1 = (bf16[4,1,32,256]{3,2,1,0:T(8,128)(2,1)S(1)}, bf16[4,1,32,256]{3,2,1,0:T(8,128)(2,1)S(1)}, u32[]{:S(2)}, u32[]{:S(2)}) collective-permute-start(bf16[4,1,32,256]{3,2,1,0:T(8,128)(2,1)S(1)} %get-tuple-element.30), channel_id=1, source_target_pairs={{1,0},{2,1},{3,2},{5,4},{6,5},{7,6},{9,8},{10,9},{11,10},{13,12},{... | collective-permute-start | bytes 196616 | tf_op jit(solution)/shard_map/ppermute | solution.py:15
  16.4 19.7 %collective-permute-start.3 = (bf16[2,8,64,256]{3,2,1,0:T(8,128)(2,1)}, bf16[2,8,64,256]{3,2,1,0:T(8,128)(2,1)}, u32[]{:S(2)}, u32[]{:S(2)}) collective-permute-start(bf16[2,8,64,256]{3,2,1,0:T(8,128)(2,1)} %slice_bitcast_fusion), channel_id=1, source_target_pairs={{4,0},{8,4},{12,8},{5,1},{9,5},{13,9},{6,2},{10,6},{14,10},{7,3},{... | collective-permute-start | bytes 1572872 | tf_op jit(solution)/shard_map/ppermute | solution.py:23
  23.3 4.2 %copy-start.2 = (bf16[3,3,256,256]{3,2,1,0:T(8,128)(2,1)S(1)}, bf16[3,3,256,256]{3,2,1,0:T(8,128)(2,1)}, u32[]{:S(2)}) copy-start(bf16[3,3,256,256]{3,2,1,0:T(8,128)(2,1)} %param.5) | copy-start | bytes 3538948
  31.1 4.0 %copy-start = (bf16[1,4,8,64,256]{4,3,2,1,0:T(8,128)(2,1)S(1)}, bf16[1,4,8,64,256]{4,3,2,1,0:T(8,128)(2,1)}, u32[]{:S(2)}) copy-start(bf16[1,4,8,64,256]{4,3,2,1,0:T(8,128)(2,1)} %param.7) | copy-start | bytes 3145732
  31.8 3.8 %copy-start.4 = (bf16[3,256,256]{2,1,0:T(8,128)(2,1)S(1)}, bf16[3,256,256]{2,1,0:T(8,128)(2,1)}, u32[]{:S(2)}) copy-start(bf16[3,256,256]{2,1,0:T(8,128)(2,1)} %param.6) | copy-start | bytes 1179652
  31.9 18.8 %collective-permute-start.2 = (bf16[2,8,64,256]{3,2,1,0:T(8,128)(2,1)S(1)}, bf16[2,8,64,256]{3,2,1,0:T(8,128)(2,1)S(1)}, u32[]{:S(2)}, u32[]{:S(2)}) collective-permute-start(bf16[2,8,64,256]{3,2,1,0:T(8,128)(2,1)S(1)} %bitcast.235), channel_id=1, source_target_pairs={{0,4},{4,8},{8,12},{1,5},{5,9},{9,13},{2,6},{6,10},{10,14},{3,7},{... | collective-permute-start | bytes 1572872 | tf_op jit(solution)/shard_map/ppermute | solution.py:23
  36.0 1.8 copy-start.1
  40.6 14.7 %collective-permute-start.4 = (bf16[4,1,64,256]{3,2,1,0:T(8,128)(2,1)}, bf16[4,1,64,256]{3,2,1,0:T(8,128)(2,1)S(1)}, u32[]{:S(2)}, u32[]{:S(2)}) collective-permute-start(bf16[4,1,64,256]{3,2,1,0:T(8,128)(2,1)} %get-tuple-element.27), channel_id=1, source_target_pairs={{0,1},{1,2},{2,3},{4,5},{5,6},{6,7},{8,9},{9,10},{10,11},{12,13},{... | collective-permute-start | bytes 393224 | tf_op jit(solution)/shard_map/ppermute | solution.py:12
  45.2 10.2 %collective-permute-start.5 = (bf16[4,1,64,256]{3,2,1,0:T(8,128)(2,1)}, bf16[4,1,64,256]{3,2,1,0:T(8,128)(2,1)S(1)}, u32[]{:S(2)}, u32[]{:S(2)}) collective-permute-start(bf16[4,1,64,256]{3,2,1,0:T(8,128)(2,1)} %get-tuple-element.28), channel_id=1, source_target_pairs={{1,0},{2,1},{3,2},{5,4},{6,5},{7,6},{9,8},{10,9},{11,10},{13,12},{... | collective-permute-start | bytes 393224 | tf_op jit(solution)/shard_map/ppermute | solution.py:15
  50.6 1.4 copy-start.3
  196.5 3.3 %copy-start.5 = (f32[3,256,256]{2,1,0:T(8,128)S(1)}, f32[3,256,256]{2,1,0:T(8,128)}, u32[]{:S(2)}) copy-start(f32[3,256,256]{2,1,0:T(8,128)} %get-tuple-element.36) | copy-start | bytes 2359300
Sparse Core Ops, SparseCore 0:
  55.4 141.0 all-reduce.4
where the time goes:
time: 208 us
  waiting for transfers between devices  128 us (62%)
  matrix products  21.2 us (10%)
  local copies, waits for them, and re-layouts  19.1 us (9%)
  starting transfers between devices  16.9 us (8%)
  between operations  14.5 us (7%)
  other arithmetic  7.53 us (4%)
    psum x1, waiting for transfers between devices, on_device(): lax.psum((spatial_grad, temporal_grad), ('dp', 'tm', 'height'))  128 us
    ppermute x2, starting transfers between devices, extended(): lax.ppermute(lax.slice_in_dim(block, block.shape[dim] - width, None, axis...  9.46 us
    unnamed x16, local copies, waits for them, and re-layouts  5.29 us
    dot_general x3, matrix products, on_device(): jnp.dot(grad_ext[k:k + frames].reshape(-1, chan), temporal_weight[k].T, p...  4.56 us
    slice x2, local copies, waits for them, and re-layouts, spatial_apply(): piece = padded[:, i:i + rows, j:j + cols, :].reshape(-1, chan)  4.54 us
    ppermute x2, starting transfers between devices, shifted(): return lax.ppermute(block, axis, route)  4.49 us
    dot_general x9, matrix products, on_device(): lax.dot_general(piece, pre_grad, (((0,), (0,)), ((), ())), preferred_elem...  4.39 us
    dot_general x9, matrix products, on_device(): jnp.dot(piece, spatial_weight[i, j].T, preferred_element_type=jnp.float32)  4.3 us
  transfers between devices with their start and end apart: 7, of which 1 were waited for; matrix products, arithmetic and copies ran while one was open for 20% of the time, Pallas kernels for 0%

commit v1 on v0

--- a/solution.py
+++ b/solution.py
@@ -1,7 +1,51 @@
+import functools
+
 import jax
 import jax.numpy as jnp
 from jax import lax
+from jax.sharding import Mesh
 from jax.sharding import PartitionSpec as P
+
+
+class Bits:
+    def __init__(self, mesh):
+        self.axes = {}
+        for name in mesh.axis_names:
+            count = mesh.shape[name].bit_length() - 1
+            self.axes[name] = tuple(f"{name}{bit}" for bit in reversed(range(count)))
+        names = [bit for bits in self.axes.values() for bit in bits]
+        self.mesh = Mesh(mesh.devices.reshape([2] * len(names)), tuple(names))
+        self.core = next((n for n in names if self.same_chip(n)), self.axes["tm"][-1])
+        self.near = []
+        for bits in self.axes.values():
+            self.near += [b for b in bits if b != self.core][-1:]
+        self.far = [n for n in names if n != self.core and n not in self.near]
+
+    def same_chip(self, name):
+        at = [1 if n == name else 0 for n in self.mesh.axis_names]
+        here = self.mesh.devices[tuple([0] * len(at))]
+        there = self.mesh.devices[tuple(at)]
+        return tuple(getattr(here, "coords", (0,))) == tuple(getattr(there, "coords", (1,)))
+
+    def swap(self, block, axis):
+        return lax.ppermute(block, axis, [(0, 1), (1, 0)])
+
+    def reduce(self, pieces):
+        near, parts = tuple(self.near), pieces.shape[1]
+        on_core = lax.axis_index(self.core) == 1
+        mine = jnp.where(on_core, pieces[1], pieces[0])
+        other = jnp.where(on_core, pieces[0], pieces[1])
+        kept = (mine + self.swap(other, self.core)).astype(jnp.bfloat16)
+        got = lax.all_to_all(kept, near, 0, 0, tiled=True).astype(jnp.float32)
+        total = got.sum(0)
+        for axis in self.far:
+            own = total.astype(jnp.bfloat16)
+            total = own.astype(jnp.float32) + self.swap(own, axis).astype(jnp.float32)
+        total = total.astype(jnp.bfloat16)
+        spread = jnp.broadcast_to(total, (parts,) + total.shape)
+        half = lax.all_to_all(spread, near, 0, 0, tiled=True)
+        theirs = self.swap(half, self.core)
+        return jnp.stack([jnp.where(on_core, theirs, half), jnp.where(on_core, half, theirs)])
 
 
 def extended(block, sides, width):
@@ -33,18 +77,18 @@
     return total
 
 
-def on_device(low_frames, spatial_weight, temporal_weight, cotangent):
+def on_device(bits, low_frames, spatial_weight, temporal_weight, cotangent):
     low = low_frames[0]
     grad_out = cotangent[0]
     frames, rows_low, cols_low, chan = low.shape
     rows = 2 * rows_low
     cols = 2 * cols_low
-    low_ext = extended(low, (("height", 1),), 1)
+    low_ext = extended(low, ((bits.axes["height"], 1),), 1)
     upsampled = jnp.repeat(jnp.repeat(low_ext, 2, axis=1), 2, axis=2)[:, 1:-1]
     padded = jnp.pad(upsampled, ((0, 0), (0, 0), (1, 1), (0, 0)))
     pre = spatial_apply(padded, spatial_weight, rows, cols)
     act = jax.nn.silu(pre).astype(jnp.bfloat16).reshape(frames, rows, cols, chan)
-    earlier = shifted(act[frames - 2 :], "tm", 1)
+    earlier = shifted(act[frames - 2 :], bits.axes["tm"], 1)
     act_ext = jnp.concatenate([earlier, act], 0)
     mixed = padded[:, 1:-1, 1:-1, :].reshape(-1, chan).astype(jnp.float32)
     for k in range(3):
@@ -54,7 +98,7 @@
             preferred_element_type=jnp.float32,
         )
     section_out = mixed.astype(jnp.bfloat16).reshape(1, frames, rows, cols, chan)
-    later = shifted(grad_out[:2], "tm", -1)
+    later = shifted(grad_out[:2], bits.axes["tm"], -1)
     grad_ext = jnp.concatenate([grad_out, later], 0)
     grad_flat = grad_out.reshape(-1, chan)
     act_grad = jnp.zeros((frames * rows * cols, chan), jnp.float32)
@@ -67,8 +111,8 @@
         )
         tgrads.append(
             lax.dot_general(
-                act_ext[2 - k : 2 - k + frames].reshape(-1, chan),
-                grad_flat,
+                act.reshape(-1, chan),
+                grad_ext[k : k + frames].reshape(-1, chan),
                 (((0,), (0,)), ((), ())),
                 preferred_element_type=jnp.float32,
             )
@@ -86,7 +130,7 @@
                 )
             )
     spatial_grad = jnp.stack(sgrads).reshape(3, 3, chan, chan)
-    grad_rows = extended(pre_grad.reshape(frames, rows, cols, chan), (("height", 1),), 1)
+    grad_rows = extended(pre_grad.reshape(frames, rows, cols, chan), ((bits.axes["height"], 1),), 1)
     grad_pad = jnp.pad(grad_rows, ((0, 0), (0, 0), (1, 1), (0, 0)))
     total = grad_flat.astype(jnp.float32)
     for i in range(3):
@@ -98,13 +142,22 @@
     input_grad = (
         total.reshape(frames, rows_low, 2, cols_low, 2, chan).sum(axis=(2, 4)).astype(jnp.bfloat16)
     )
-    spatial_grad, temporal_grad = lax.psum((spatial_grad, temporal_grad), ("dp", "tm", "height"))
+    taps = jnp.concatenate([spatial_grad.reshape(9, chan, chan), temporal_grad])
+    parts = 1 << len(bits.near)
+    pieces = taps.reshape(12, 2, parts, chan // (2 * parts), chan).transpose(1, 2, 0, 3, 4)
+    pieces = bits.reduce(pieces).astype(jnp.float32)
+    taps = pieces.transpose(2, 0, 1, 3, 4).reshape(12, chan, chan)
+    spatial_grad, temporal_grad = taps[:9].reshape(3, 3, chan, chan), taps[9:]
     return (section_out, input_grad[None], spatial_grad, temporal_grad)
 
 
 def solution(mesh):
-    in_specs = (P("dp", "tm", "height", None, None), P(), P(), P("dp", "tm", "height", None, None))
-    out_specs = (P("dp", "tm", "height", None, None), P("dp", "tm", "height", None, None), P(), P())
+    bits = Bits(mesh)
+    block = P(*(bits.axes[name] for name in ("dp", "tm", "height")), None, None)
     return jax.shard_map(
-        on_device, mesh=mesh, in_specs=in_specs, out_specs=out_specs, check_vma=False
+        functools.partial(on_device, bits),
+        mesh=bits.mesh,
+        in_specs=(block, P(), P(), block),
+        out_specs=(block, block, P(), P()),
+        check_vma=False,
     )

time: 208 us -> 160 us (0.77)
  waiting for transfers between devices: 128 us -> 5.25 us
  matrix products: 21.2 us -> 60.5 us
  local copies, waits for them, and re-layouts: 19.1 us -> 44 us
  starting transfers between devices: 16.9 us -> 31.9 us
  between operations: 14.5 us -> 1.16 us
  other arithmetic: 7.53 us -> 16.1 us
    psum x1 -> x0, waiting for transfers between devices: 128 us -> none  [on_device(): lax.psum((spatial_grad, temporal_grad), ('dp', 'tm', 'height'))]
    dot_general x9, matrix products: 4.22 us -> 29.1 us  [spatial_apply(): jnp.dot(piece, weights[i, j], preferred_element_type=jnp.float32)]
    dot_general x9, matrix products: 4.3 us -> 16.3 us  [on_device(): jnp.dot(piece, spatial_weight[i, j].T, preferred_element_type=jnp.float32)]
    reshape x0 -> x8, local copies, waits for them, and re-layouts: none -> 11.5 us  [spatial_apply(): piece = padded[:, i:i + rows, j:j + cols, :].reshape(-1, chan)]
    all_to_all x0 -> x2, starting transfers between devices: none -> 11.2 us  [the longest x1 6.72 us: reduce(): got = lax.all_to_all(kept, near, 0, 0, tiled=True).astype(jnp.float32)]
    ppermute x0 -> x3, starting transfers between devices: none -> 3.85 us  [swap(): return lax.ppermute(block, axis, [(0, 1), (1, 0)])]
    concatenate x3, other arithmetic: 0.99 us -> 4.31 us  [extended(): block = jnp.concatenate([low, block, high], axis=dim)]
    all_to_all x0 -> x2, waiting for transfers between devices: none -> 3.09 us  [the longest x1 3.08 us: reduce(): half = lax.all_to_all(spread, near, 0, 0, tiled=True)]
  transfers between devices with their start and end apart: 7 -> 11, of which waited for: 1 -> 2; matrix products, arithmetic and copies ran while one was open for 20% -> 62% of each run, Pallas kernels for 0% -> 0%
where the time goes in v1:
time: 160 us; the launch traced here: 159 us
  matrix products  60.5 us (38%)
  local copies, waits for them, and re-layouts  44 us (28%)
  starting transfers between devices  31.9 us (20%)
  other arithmetic  16.1 us (10%)
  waiting for transfers between devices  5.25 us (3%)
    dot_general x9, matrix products, spatial_apply(): jnp.dot(piece, weights[i, j], preferred_element_type=jnp.float32)  29.1 us
    dot_general x9, matrix products, on_device(): jnp.dot(piece, spatial_weight[i, j].T, preferred_element_type=jnp.float32)  16.3 us
    reshape x8, local copies, waits for them, and re-layouts, spatial_apply(): piece = padded[:, i:i + rows, j:j + cols, :].reshape(-1, chan)  11.5 us
    ppermute x2, starting transfers between devices, extended(): lax.ppermute(lax.slice_in_dim(block, block.shape[dim] - width, None, axis...  10.1 us
    all_to_all x1, starting transfers between devices, reduce(): got = lax.all_to_all(kept, near, 0, 0, tiled=True).astype(jnp.float32)  6.72 us
    slice x2, local copies, waits for them, and re-layouts, spatial_apply(): piece = padded[:, i:i + rows, j:j + cols, :].reshape(-1, chan)  6.42 us
    dot_general x3, matrix products, on_device(): jnp.dot(act_ext[2 - k:2 - k + frames].reshape(-1, chan), temporal_weight[...  5.2 us
    dot_general x3, matrix products, on_device(): jnp.dot(grad_ext[k:k + frames].reshape(-1, chan), temporal_weight[k].T, p...  4.54 us
  transfers between devices with their start and end apart: 11, of which 2 were waited for; matrix products, arithmetic and copies ran while one was open for 62% of the time, Pallas kernels for 0%

profile of v1, /device:TPU:0, one launch (start us, length us, event | category | flops | bytes accessed | tf_op | source)
XLA Modules:
  0.0 158.9 jit_solution(5716340393944241478)
XLA Ops:
  1.5 4.9 %collective-permute-start = (bf16[4,1,32,256]{3,2,1,0:T(8,128)(2,1)S(1)}, bf16[4,1,32,256]{3,2,1,0:T(8,128)(2,1)S(1)}, u32[]{:S(2)}, u32[]{:S(2)}) collective-permute-start(bf16[4,1,32,256]{3,2,1,0:T(8,128)(2,1)S(1)} %get-tuple-element.29), channel_id=1, source_target_pairs={{0,1},{1,2},{2,3},{4,5},{5,6},{6,7},{8,9},{9,10},{10,11},{12,13},{... | collective-permute-start | bytes 196616 | tf_op jit(solution)/shard_map/ppermute | solution.py:56
  7.9 1.9 %slice_bitcast_fusion = bf16[2,8,64,256]{3,2,1,0:T(8,128)(2,1)} fusion(bf16[1,4,8,64,256]{4,3,2,1,0:T(8,128)(2,1)} %param.7), kind=kLoop, calls=%fused_computation.98 | loop fusion | bytes 1048576 | tf_op jit(solution)/shard_map/slice | solution.py:101
  11.1 3.0 %fusion.45 = f32[2048,256]{1,0:T(8,128)} fusion(bf16[2048,256]{1,0:T(8,128)(2,1)} %bitcast.293, bf16[3,256,256]{2,1,0:T(8,128)(2,1)} %param.6), kind=kOutput, calls=%fused_computation.106 | convolution fusion | flops 268435456 | bytes 3276800 | tf_op jit(solution)/shard_map/dot_general | solution.py:107
  14.3 2.6 %broadcast_in_dim.11 = bf16[4,12,32,2,256]{4,3,2,1,0:T(2,128)(2,1)} broadcast(bf16[4,12,32,256]{3,2,1,0:T(8,128)(2,1)S(1)} %bitcast.345), dimensions={0,1,2,4} | broadcast | bytes 2359296 | tf_op jit(solution)/shard_map/broadcast_in_dim | solution.py:87
  16.9 2.5 %reshape.218 = bf16[4,12,64,256]{3,2,1,0:T(8,128)(2,1)S(1)} reshape(bf16[4,12,32,2,256]{4,3,2,1,0:T(2,128)(2,1)} %broadcast_in_dim.11) | data formatting | bytes 3145728 | tf_op jit(solution)/shard_map/reshape | solution.py:87
  19.5 1.7 %fusion.93 = (bf16[4,8,64,256]{3,2,1,0:T(8,128)(2,1)}, bf16[4,8,64,256]{3,2,1,0:T(8,128)(2,1)}, bf16[4,8,64,256]{3,2,1,0:T(8,128)(2,1)S(1)}) fusion(bf16[4,12,64,256]{3,2,1,0:T(8,128)(2,1)S(1)} %reshape.218), kind=kLoop, calls=%fused_computation.154 | loop fusion | bytes 6291456 | tf_op jit(solution)/shard_map/slice | solution.py:75
  21.2 4.7 %pad_slice_fusion.4 = (bf16[4,8,64,256]{3,2,1,0:T(8,128)(2,1)}, bf16[4,8,64,256]{3,2,1,0:T(8,128)(2,1)}, bf16[4,8,64,256]{3,2,1,0:T(8,128)(2,1)}, bf16[4,8,64,25...) fusion(bf16[4,10,64,256]{3,2,1,0:T(8,128)(2,1)S(1)} %slice.230), kind=kLoop, calls=%fused_computation.90 | loop fusion | bytes 7602176 | tf_op jit(solution)/shard_map/slice | solution.py:75
  25.9 1.4 copy.55
  27.3 2.7 %fusion.67 = f32[2048,256]{1,0:T(8,128)} fusion(bf16[2048,256]{1,0:T(8,128)(2,1)S(1)} %bitcast.312, bf16[3,3,256,256]{3,2,1,0:T(8,128)(2,1)} %param.5), kind=kOutput, calls=%fused_computation.128 | convolution fusion | flops 268435456 | bytes 3276800 | tf_op jit(solution)/shard_map/dot_general | solution.py:76
  30.1 1.4 copy.56
  31.5 3.5 %convolution_add_fusion.19 = f32[2048,256]{1,0:T(8,128)} fusion(f32[2048,256]{1,0:T(8,128)} %fusion.67, bf16[2048,256]{1,0:T(8,128)(2,1)S(1)} %bitcast.310, bf16[3,3,256,256]{3,2,1,0:T(8,128)(2,1)} %param.5), kind=kOutput, calls=%fused_computation.26 | convolution fusion | flops 268959744 | bytes 5373952 | tf_op jit(solution)/shard_map/dot_general | solution.py:76
  35.0 1.4 copy.57
  36.5 3.5 %convolution_add_fusion.18 = f32[2048,256]{1,0:T(8,128)} fusion(f32[2048,256]{1,0:T(8,128)} %convolution_add_fusion.19, bf16[2048,256]{1,0:T(8,128)(2,1)S(1)} %bitcast.320, bf16[3,3,256,256]{3,2,1,0:T(8,128)(2,1)} %param.5), kind=kOutput, calls=%fused_computation.25 | convolution fusion | flops 268959744 | bytes 5373952 | tf_op jit(solution)/shard_map/dot_general | solution.py:76
  40.0 1.5 copy.58
  41.4 3.5 %convolution_add_fusion.17 = f32[2048,256]{1,0:T(8,128)} fusion(f32[2048,256]{1,0:T(8,128)} %convolution_add_fusion.18, bf16[2048,256]{1,0:T(8,128)(2,1)S(1)} %bitcast.318, bf16[3,3,256,256]{3,2,1,0:T(8,128)(2,1)} %param.5), kind=kOutput, calls=%fused_computation.24 | convolution fusion | flops 268959744 | bytes 5373952 | tf_op jit(solution)/shard_map/dot_general | solution.py:76
  44.9 1.4 copy.60
  46.4 2.1 %convolution_add_fusion.16 = f32[2048,256]{1,0:T(8,128)S(1)} fusion(f32[2048,256]{1,0:T(8,128)} %convolution_add_fusion.17, bf16[2048,256]{1,0:T(8,128)(2,1)S(1)} %bitcast.300, bf16[3,3,256,256]{3,2,1,0:T(8,128)(2,1)} %param.5), kind=kOutput, calls=%fused_computation.23 | convolution fusion | flops 268959744 | bytes 5373952 | tf_op jit(solution)/shard_map/dot_general | solution.py:76
  48.5 2.7 %convolution_add_fusion.15 = f32[2048,256]{1,0:T(8,128)} fusion(f32[2048,256]{1,0:T(8,128)S(1)} %convolution_add_fusion.16, bf16[2048,256]{1,0:T(8,128)(2,1)S(1)} %bitcast.316, bf16[3,3,256,256]{3,2,1,0:T(8,128)(2,1)} %param.5), kind=kOutput, calls=%fused_computation.22 | convolution fusion | flops 268959744 | bytes 5373952 | tf_op jit(solution)/shard_map/dot_general | solution.py:76
  52.6 3.5 %convolution_add_fusion.14 = f32[2048,256]{1,0:T(8,128)} fusion(f32[2048,256]{1,0:T(8,128)} %convolution_add_fusion.15, bf16[2048,256]{1,0:T(8,128)(2,1)S(1)} %bitcast.314, bf16[3,3,256,256]{3,2,1,0:T(8,128)(2,1)} %param.5), kind=kOutput, calls=%fused_computation.21 | convolution fusion | flops 268959744 | bytes 5373952 | tf_op jit(solution)/shard_map/dot_general | solution.py:76
  56.1 1.4 copy.62
  57.6 3.5 %convolution_add_fusion.13 = f32[2048,256]{1,0:T(8,128)} fusion(f32[2048,256]{1,0:T(8,128)} %convolution_add_fusion.14, bf16[2048,256]{1,0:T(8,128)(2,1)S(1)} %bitcast.308, bf16[3,3,256,256]{3,2,1,0:T(8,128)(2,1)} %param.5), kind=kOutput, calls=%fused_computation.20 | convolution fusion | flops 268959744 | bytes 5373952 | tf_op jit(solution)/shard_map/dot_general | solution.py:76
  61.1 1.4 copy.63
  62.5 4.0 %multiply_convert_fusion = (bf16[2048,256]{1,0:T(8,128)(2,1)}, f32[2048,256]{1,0:T(8,128)}) fusion(f32[2048,256]{1,0:T(8,128)} %convolution_add_fusion.13, bf16[2048,256]{1,0:T(8,128)(2,1)S(1)} %bitcast.344, bf16[3,3,256,256]{3,2,1,0:T(8,128)(2,1)} %param.5), kind=kOutput, calls=%fused_computation.34 | convolution fusion | flops 271581184 | bytes 6422528 | tf_op jit(solution)/shard_map/dot_general | solution.py:76
  66.5 1.5 copy.59
  67.9 2.2 %fusion.9 = bf16[256,2048]{0,1:T(8,128)(2,1)S(1)} fusion(f32[2048,256]{1,0:T(8,128)} %get-tuple-element.32), kind=kLoop, calls=%fused_computation.36 | loop fusion | flops 2621440 | bytes 3145728 | tf_op jit(solution)/shard_map/convert_element_type | solution.py:90
  71.1 1.4 pad_maximum_fusion.2
  84.6 2.7 %collective-permute-start.2 = (bf16[2,8,64,256]{3,2,1,0:T(8,128)(2,1)S(1)}, bf16[2,8,64,256]{3,2,1,0:T(8,128)(2,1)S(1)}, u32[]{:S(2)}, u32[]{:S(2)}) collective-permute-start(bf16[2,8,64,256]{3,2,1,0:T(8,128)(2,1)S(1)} %bitcast.351), channel_id=1, source_target_pairs={{0,4},{4,8},{8,12},{1,5},{5,9},{9,13},{2,6},{6,10},{10,14},{3,7},{... | collective-permute-start | bytes 1572872 | tf_op jit(solution)/shard_map/ppermute | solution.py:67
  88.5 5.2 %collective-permute-start.4 = (bf16[4,1,64,256]{3,2,1,0:T(8,128)(2,1)}, bf16[4,1,64,256]{3,2,1,0:T(8,128)(2,1)}, u32[]{:S(2)}, u32[]{:S(2)}) collective-permute-start(bf16[4,1,64,256]{3,2,1,0:T(8,128)(2,1)} %get-tuple-element.27), channel_id=1, source_target_pairs={{0,1},{1,2},{2,3},{4,5},{5,6},{6,7},{8,9},{9,10},{10,11},{12,13},{... | collective-permute-start | bytes 393224 | tf_op jit(solution)/shard_map/ppermute | solution.py:56
  95.2 1.8 %convolution_add_fusion.10 = f32[2048,256]{1,0:T(8,128)} fusion(f32[2048,256]{1,0:T(8,128)S(1)} %convolution_add_fusion.11, bf16[2048,256]{1,0:T(8,128)(2,1)S(1)} %bitcast.342, bf16[3,256,256]{2,1,0:T(8,128)(2,1)S(1)} %copy-done.29), kind=kOutput, calls=%fused_computation.17 | convolution fusion | flops 268959744 | bytes 5373952 | tf_op jit(solution)/shard_map/dot_general | solution.py:95
  98.6 6.7 %all-to-all-start = ((bf16[8,12,16,256]{3,2,1,0:T(8,128)(2,1)}), bf16[8,12,16,256]{3,2,1,0:T(8,128)(2,1)}, u32[]{:S(2)}, u32[]{:S(2)}) async-start(bf16[8,12,16,256]{3,2,1,0:T(8,128)(2,1)} %copy.69), calls=%async_computation | async-start | bytes 1572864 | tf_op jit(solution)/shard_map/all_to_all | solution.py:39
  105.3 3.0 %fusion.5 = bf16[2048,256]{1,0:T(8,128)(2,1)} fusion(f32[2048,256]{1,0:T(8,128)} %convolution_add_fusion.10, bf16[2048,256]{1,0:T(8,128)(2,1)S(1)} %bitcast.340, bf16[3,256,256]{2,1,0:T(8,128)(2,1)S(1)} %copy-done.29), kind=kOutput, calls=%fused_computation.28 | convolution fusion | flops 269484032 | bytes 4325376 | tf_op jit(solution)/shard_map/dot_general | solution.py:95
  108.3 1.8 %fusion.17 = bf16[4,10,66,256]{3,2,1,0:T(8,128)(2,1)S(1)} fusion(bf16[4,1,64,256]{3,2,1,0:T(8,128)(2,1)} %collective-permute-done.5, bf16[4,8,64,256]{3,2,1,0:T(8,128)(2,1)S(1)} %bitcast.291, bf16[4,1,64,256]{3,2,1,0:T(8,128)(2,1)} %collective-permute-done.4), kind=kLoop, calls=%fused_computation.50 | loop fusion | flops 8110080 | bytes 2662400 | tf_op jit(solution)/shard_map/concatenate | solution.py:60
  110.0 2.6 %fusion.94 = (bf16[4,8,64,256]{3,2,1,0:T(8,128)(2,1)}, bf16[4,8,64,256]{3,2,1,0:T(8,128)(2,1)}, bf16[4,8,64,256]{3,2,1,0:T(8,128)(2,1)}, bf16[4,8,64,256]{3,2,1,...) fusion(bf16[4,10,66,256]{3,2,1,0:T(8,128)(2,1)S(1)} %fusion.17), kind=kLoop, calls=%fused_computation.155 | loop fusion | bytes 12582912 | tf_op jit(solution)/shard_map/slice | solution.py:138
  112.7 2.7 %fusion.61 = f32[2048,256]{1,0:T(8,128)} fusion(bf16[2048,256]{1,0:T(8,128)(2,1)S(1)} %bitcast.323, bf16[3,3,256,256]{3,2,1,0:T(8,128)(2,1)} %param.5), kind=kOutput, calls=%fused_computation.122 | convolution fusion | flops 268435456 | bytes 3276800 | tf_op jit(solution)/shard_map/dot_general | solution.py:139
  115.4 2.7 %convolution_add_fusion.6 = f32[2048,256]{1,0:T(8,128)} fusion(bf16[2048,256]{1,0:T(8,128)(2,1)S(1)} %bitcast.341, bf16[2048,256]{1,0:T(8,128)(2,1)S(1)} %bitcast.296, bf16[3,3,256,256]{3,2,1,0:T(8,128)(2,1)} %param.5), kind=kOutput, calls=%fused_computation.12 | convolution fusion | flops 269484032 | bytes 4325376 | tf_op jit(solution)/shard_map/dot_general | solution.py:139
  119.3 2.7 %collective-permute-start.7 = (bf16[12,16,256]{2,1,0:T(8,128)(2,1)S(1)}, bf16[12,16,256]{2,1,0:T(8,128)(2,1)S(1)}, u32[]{:S(2)}, u32[]{:S(2)}) collective-permute-start(bf16[12,16,256]{2,1,0:T(8,128)(2,1)S(1)} %reduce_sum.22), channel_id=1, source_target_pairs={{0,2},{2,0},{1,3},{3,1},{4,6},{6,4},{5,7},{7,5},{8,10},{10,8},{9,1... | collective-permute-start | bytes 294920 | tf_op jit(solution)/shard_map/ppermute | solution.py:31
  122.0 2.5 %pad_maximum_fusion = (bf16[4,8,64,256]{3,2,1,0:T(8,128)(2,1)}, bf16[4,8,64,256]{3,2,1,0:T(8,128)(2,1)}) fusion(bf16[4,8,64,256]{3,2,1,0:T(8,128)(2,1)S(1)} %bitcast.292, bf16[4,1,64,256]{3,2,1,0:T(8,128)(2,1)} %collective-permute-done.4, bf16[4,1,64,256]{3,2,1,0:T(8,128)(2,1)} %collective-permute-done.5), kind=kLoop, calls=%fused_computation.77 | loop fusion | flops 1048576 | bytes 3407872 | tf_op jit(solution)/shard_map/concatenate | solution.py:60
  124.5 2.1 %collective-permute-done.7 = bf16[12,16,256]{2,1,0:T(8,128)(2,1)S(1)} collective-permute-done((bf16[12,16,256]{2,1,0:T(8,128)(2,1)S(1)}, bf16[12,16,256]{2,1,0:T(8,128)(2,1)S(1)}, u32[]{:S(2)}, u32[]{:S(2)}) %collective-permute-start.7) | collective-permute-done | bytes 98336 | tf_op jit(solution)/shard_map/ppermute | solution.py:31
  127.6 4.5 %all-to-all-start.1 = ((bf16[8,12,16,256]{3,2,1,0:T(8,128)(2,1)}), bf16[8,12,16,256]{3,2,1,0:T(8,128)(2,1)}, u32[]{:S(2)}, u32[]{:S(2)}) async-start(bf16[8,12,16,256]{3,2,1,0:T(8,128)(2,1)} %broadcast_in_dim.12), calls=%async_computation.1 | async-start | bytes 1572864 | tf_op jit(solution)/shard_map/all_to_all | solution.py:46
  132.1 2.5 %fusion.2 = f32[2048,256]{1,0:T(8,128)S(1)} fusion(f32[2048,256]{1,0:T(8,128)S(1)} %copy-done.10, f32[2048,256]{1,0:T(8,128)} %convolution_add_fusion.6, bf16[2048,256]{1,0:T(8,128)(2,1)} %bitcast.327, bf16[3,3,256,256]{3,2,1,0:T(8,128)(2,1)} %param.5), kind=kOutput, calls=%fused_computation.11 | convolution fusion | flops 269484032 | bytes 7471104 | tf_op jit(solution)/shard_map/dot_general | solution.py:139
  136.0 1.5 convolution_add_fusion.3
  138.9 3.1 %all-to-all-done.1 = bf16[8,12,16,256]{3,2,1,0:T(8,128)(2,1)} async-done(((bf16[8,12,16,256]{3,2,1,0:T(8,128)(2,1)}), bf16[8,12,16,256]{3,2,1,0:T(8,128)(2,1)}, u32[]{:S(2)}, u32[]{:S(2)}) %all-to-all-start.1) | async-done | bytes 786464 | tf_op jit(solution)/shard_map/all_to_all | solution.py:46
  142.0 2.2 %copy.70 = bf16[8,12,16,256]{3,2,0,1:T(8,128)(2,1)} copy(bf16[8,12,16,256]{3,2,1,0:T(8,128)(2,1)} %all-to-all-done.1) | data formatting | bytes 1572864 | tf_op jit(solution)/shard_map/all_to_all | solution.py:46
  145.6 1.5 convolution_add_fusion.1
  148.4 2.2 %reshape.243 = f32[4,4,2,32,2,256]{5,4,3,2,1,0:T(2,128)} reshape(f32[2048,256]{1,0:T(8,128)S(1)} %fusion.1) | data formatting | bytes 4194304 | tf_op jit(solution)/shard_map/reshape | solution.py:143
  150.7 4.0 %reduce_sum.21 = bf16[4,4,32,256]{3,2,1,0:T(8,128)(2,1)} reduce(f32[4,4,2,32,2,256]{5,4,3,2,1,0:T(2,128)} %reshape.243, f32[]{:T(128)} %constant.14.clone.1), dimensions={2,4}, to_apply=%region_0.1 | reduce | flops 393216 | bytes 2359300 | tf_op jit(solution)/shard_map/reduce_sum | solution.py:143
  154.6 1.5 select_bitcast_fusion.2
  156.3 1.6 %slice.248 = f32[9,2,8,16,256]{4,3,2,1,0:T(8,128)} slice(f32[12,2,8,16,256]{4,3,2,1,0:T(8,128)S(1)} %convert_bitcast_fusion), slice={[0:9], [0:2], [0:8], [0:16], [0:256]} | slice | bytes 4718592 | tf_op jit(solution)/shard_map/slice | solution.py:150
  (112 shorter events, 31.2 us)
Async XLA Ops:
  1.5 12.6 %collective-permute-start = (bf16[4,1,32,256]{3,2,1,0:T(8,128)(2,1)S(1)}, bf16[4,1,32,256]{3,2,1,0:T(8,128)(2,1)S(1)}, u32[]{:S(2)}, u32[]{:S(2)}) collective-permute-start(bf16[4,1,32,256]{3,2,1,0:T(8,128)(2,1)S(1)} %get-tuple-element.29), channel_id=1, source_target_pairs={{0,1},{1,2},{2,3},{4,5},{5,6},{6,7},{8,9},{9,10},{10,11},{12,13},{... | collective-permute-start | bytes 196616 | tf_op jit(solution)/shard_map/ppermute | solution.py:56
  6.5 7.7 %copy-start.30 = (bf16[1,4,4,32,256]{4,3,2,1,0:T(8,128)(2,1)S(1)}, bf16[1,4,4,32,256]{4,3,2,1,0:T(8,128)(2,1)}, u32[]{:S(2)}) copy-start(bf16[1,4,4,32,256]{4,3,2,1,0:T(8,128)(2,1)} %param.4) | copy-start | bytes 786436
  6.5 7.6 %collective-permute-start.1 = (bf16[4,1,32,256]{3,2,1,0:T(8,128)(2,1)S(1)}, bf16[4,1,32,256]{3,2,1,0:T(8,128)(2,1)S(1)}, u32[]{:S(2)}, u32[]{:S(2)}) collective-permute-start(bf16[4,1,32,256]{3,2,1,0:T(8,128)(2,1)S(1)} %get-tuple-element.30), channel_id=1, source_target_pairs={{1,0},{2,1},{3,2},{5,4},{6,5},{7,6},{9,8},{10,9},{11,10},{13,12},{... | collective-permute-start | bytes 196616 | tf_op jit(solution)/shard_map/ppermute | solution.py:59
  9.8 61.2 %collective-permute-start.3 = (bf16[2,8,64,256]{3,2,1,0:T(8,128)(2,1)}, bf16[2,8,64,256]{3,2,1,0:T(8,128)(2,1)}, u32[]{:S(2)}, u32[]{:S(2)}) collective-permute-start(bf16[2,8,64,256]{3,2,1,0:T(8,128)(2,1)} %slice_bitcast_fusion), channel_id=1, source_target_pairs={{4,0},{8,4},{12,8},{5,1},{9,5},{13,9},{6,2},{10,6},{14,10},{7,3},{... | collective-permute-start | bytes 1572872 | tf_op jit(solution)/shard_map/ppermute | solution.py:67
  21.2 45.3 %copy-start.1 = (bf16[4,8,64,256]{3,2,1,0:T(8,128)(2,1)}, bf16[4,8,64,256]{3,2,1,0:T(8,128)(2,1)S(1)}, u32[]{:S(2)}) copy-start(bf16[4,8,64,256]{3,2,1,0:T(8,128)(2,1)S(1)} %get-tuple-element.12) | copy-start | bytes 3145732
  27.3 2.8 %copy-start.4 = (bf16[4,8,64,256]{3,2,1,0:T(8,128)(2,1)S(1)}, bf16[4,8,64,256]{3,2,1,0:T(8,128)(2,1)}, u32[]{:S(2)}) copy-start(bf16[4,8,64,256]{3,2,1,0:T(8,128)(2,1)} %get-tuple-element.11) | copy-start | bytes 3145732
  31.5 3.5 %copy-start.8 = (bf16[4,8,64,256]{3,2,1,0:T(8,128)(2,1)S(1)}, bf16[4,8,64,256]{3,2,1,0:T(8,128)(2,1)}, u32[]{:S(2)}) copy-start(bf16[4,8,64,256]{3,2,1,0:T(8,128)(2,1)} %get-tuple-element.20) | copy-start | bytes 3145732
  35.0 1.4 copy-start.9
  36.5 3.5 %copy-start.7 = (bf16[4,8,64,256]{3,2,1,0:T(8,128)(2,1)S(1)}, bf16[4,8,64,256]{3,2,1,0:T(8,128)(2,1)}, u32[]{:S(2)}) copy-start(bf16[4,8,64,256]{3,2,1,0:T(8,128)(2,1)} %get-tuple-element.21) | copy-start | bytes 3145732
  41.4 3.5 %copy-start.6 = (bf16[4,8,64,256]{3,2,1,0:T(8,128)(2,1)S(1)}, bf16[4,8,64,256]{3,2,1,0:T(8,128)(2,1)}, u32[]{:S(2)}) copy-start(bf16[4,8,64,256]{3,2,1,0:T(8,128)(2,1)} %get-tuple-element.22) | copy-start | bytes 3145732
  48.5 2.8 %copy-start.5 = (bf16[4,8,64,256]{3,2,1,0:T(8,128)(2,1)S(1)}, bf16[4,8,64,256]{3,2,1,0:T(8,128)(2,1)}, u32[]{:S(2)}) copy-start(bf16[4,8,64,256]{3,2,1,0:T(8,128)(2,1)} %get-tuple-element.23) | copy-start | bytes 3145732
  52.6 3.5 %copy-start.3 = (bf16[4,8,64,256]{3,2,1,0:T(8,128)(2,1)S(1)}, bf16[4,8,64,256]{3,2,1,0:T(8,128)(2,1)}, u32[]{:S(2)}) copy-start(bf16[4,8,64,256]{3,2,1,0:T(8,128)(2,1)} %get-tuple-element.10) | copy-start | bytes 3145732
  57.6 3.5 %copy-start.27 = (bf16[4,8,64,256]{3,2,1,0:T(8,128)(2,1)S(1)}, bf16[4,8,64,256]{3,2,1,0:T(8,128)(2,1)}, u32[]{:S(2)}) copy-start(bf16[4,8,64,256]{3,2,1,0:T(8,128)(2,1)} %get-tuple-element.19) | copy-start | bytes 3145732
  67.9 3.1 %copy-start = (bf16[1,4,8,64,256]{4,3,2,1,0:T(8,128)(2,1)S(1)}, bf16[1,4,8,64,256]{4,3,2,1,0:T(8,128)(2,1)}, u32[]{:S(2)}) copy-start(bf16[1,4,8,64,256]{4,3,2,1,0:T(8,128)(2,1)} %param.7) | copy-start | bytes 3145732
  71.0 1.8 %copy-start.11 = (f32[2048,256]{1,0:T(8,128)S(1)}, f32[2048,256]{1,0:T(8,128)}, u32[]{:S(2)}) copy-start(f32[2048,256]{1,0:T(8,128)} %fusion.45) | copy-start | bytes 6291460
  71.0 1.9 %copy-start.29 = (bf16[3,256,256]{2,1,0:T(8,128)(2,1)S(1)}, bf16[3,256,256]{2,1,0:T(8,128)(2,1)}, u32[]{:S(2)}) copy-start(bf16[3,256,256]{2,1,0:T(8,128)(2,1)} %param.6) | copy-start | bytes 1179652
  72.9 1.6 %copy-start.28 = (f32[2048,256]{1,0:T(8,128)S(1)}, f32[2048,256]{1,0:T(8,128)}, u32[]{:S(2)}) copy-start(f32[2048,256]{1,0:T(8,128)} %get-tuple-element.32) | copy-start | bytes 6291460
  74.5 1.2 copy-start.16
  75.5 1.3 copy-start.17
  75.7 1.6 copy-start.19
  76.8 1.3 copy-start.20
  77.3 1.3 copy-start.26
  78.1 1.3 copy-start.18
  78.6 1.3 copy-start.21
  79.4 1.3 copy-start.22
  79.9 1.3 copy-start.24
  83.0 1.6 copy-start.12
  83.0 4.3 %copy-start.2 = (bf16[4,8,64,256]{3,2,1,0:T(8,128)(2,1)S(1)}, bf16[4,8,64,256]{3,2,1,0:T(8,128)(2,1)}, u32[]{:S(2)}) copy-start(bf16[4,8,64,256]{3,2,1,0:T(8,128)(2,1)} %copy-done.1) | copy-start | bytes 3145732
  83.4 13.6 %collective-permute-start.6 = (f32[8,12,16,256]{3,2,0,1:T(8,128)S(1)}, f32[8,12,16,256]{3,2,0,1:T(8,128)S(1)}, u32[]{:S(2)}, u32[]{:S(2)}) collective-permute-start(f32[8,12,16,256]{3,2,0,1:T(8,128)S(1)} %select_bitcast_fusion), channel_id=1, source_target_pairs={{0,4},{4,0},{1,5},{5,1},{2,6},{6,2},{3,7},{7,3},{8,12},{12,8},{9,1... | collective-permute-start | bytes 4718600 | tf_op jit(solution)/shard_map/ppermute | solution.py:31
  84.6 10.4 %collective-permute-start.2 = (bf16[2,8,64,256]{3,2,1,0:T(8,128)(2,1)S(1)}, bf16[2,8,64,256]{3,2,1,0:T(8,128)(2,1)S(1)}, u32[]{:S(2)}, u32[]{:S(2)}) collective-permute-start(bf16[2,8,64,256]{3,2,1,0:T(8,128)(2,1)S(1)} %bitcast.351), channel_id=1, source_target_pairs={{0,4},{4,8},{8,12},{1,5},{5,9},{9,13},{2,6},{6,10},{10,14},{3,7},{... | collective-permute-start | bytes 1572872 | tf_op jit(solution)/shard_map/ppermute | solution.py:67
  88.5 19.8 %collective-permute-start.4 = (bf16[4,1,64,256]{3,2,1,0:T(8,128)(2,1)}, bf16[4,1,64,256]{3,2,1,0:T(8,128)(2,1)}, u32[]{:S(2)}, u32[]{:S(2)}) collective-permute-start(bf16[4,1,64,256]{3,2,1,0:T(8,128)(2,1)} %get-tuple-element.27), channel_id=1, source_target_pairs={{0,1},{1,2},{2,3},{4,5},{5,6},{6,7},{8,9},{9,10},{10,11},{12,13},{... | collective-permute-start | bytes 393224 | tf_op jit(solution)/shard_map/ppermute | solution.py:56
  93.7 14.6 %collective-permute-start.5 = (bf16[4,1,64,256]{3,2,1,0:T(8,128)(2,1)}, bf16[4,1,64,256]{3,2,1,0:T(8,128)(2,1)}, u32[]{:S(2)}, u32[]{:S(2)}) collective-permute-start(bf16[4,1,64,256]{3,2,1,0:T(8,128)(2,1)} %get-tuple-element.28), channel_id=1, source_target_pairs={{1,0},{2,1},{3,2},{5,4},{6,5},{7,6},{9,8},{10,9},{11,10},{13,12},{... | collective-permute-start | bytes 393224 | tf_op jit(solution)/shard_map/ppermute | solution.py:59
  98.6 19.5 %all-to-all-start = ((bf16[8,12,16,256]{3,2,1,0:T(8,128)(2,1)}), bf16[8,12,16,256]{3,2,1,0:T(8,128)(2,1)}, u32[]{:S(2)}, u32[]{:S(2)}) async-start(bf16[8,12,16,256]{3,2,1,0:T(8,128)(2,1)} %copy.69), calls=%async_computation | async-start | bytes 1572864 | tf_op jit(solution)/shard_map/all_to_all | solution.py:39
  119.3 7.3 %collective-permute-start.7 = (bf16[12,16,256]{2,1,0:T(8,128)(2,1)S(1)}, bf16[12,16,256]{2,1,0:T(8,128)(2,1)S(1)}, u32[]{:S(2)}, u32[]{:S(2)}) collective-permute-start(bf16[12,16,256]{2,1,0:T(8,128)(2,1)S(1)} %reduce_sum.22), channel_id=1, source_target_pairs={{0,2},{2,0},{1,3},{3,1},{4,6},{6,4},{5,7},{7,5},{8,10},{10,8},{9,1... | collective-permute-start | bytes 294920 | tf_op jit(solution)/shard_map/ppermute | solution.py:31
  124.5 7.6 %copy-start.10 = (f32[2048,256]{1,0:T(8,128)S(1)}, f32[2048,256]{1,0:T(8,128)}, u32[]{:S(2)}) copy-start(f32[2048,256]{1,0:T(8,128)} %fusion.61) | copy-start | bytes 6291460
  127.6 14.4 %all-to-all-start.1 = ((bf16[8,12,16,256]{3,2,1,0:T(8,128)(2,1)}), bf16[8,12,16,256]{3,2,1,0:T(8,128)(2,1)}, u32[]{:S(2)}, u32[]{:S(2)}) async-start(bf16[8,12,16,256]{3,2,1,0:T(8,128)(2,1)} %broadcast_in_dim.12), calls=%async_computation.1 | async-start | bytes 1572864 | tf_op jit(solution)/shard_map/all_to_all | solution.py:46
  132.1 2.6 %copy-start.25 = (bf16[4,8,64,256]{3,2,1,0:T(8,128)(2,1)S(1)}, bf16[4,8,64,256]{3,2,1,0:T(8,128)(2,1)}, u32[]{:S(2)}) copy-start(bf16[4,8,64,256]{3,2,1,0:T(8,128)(2,1)} %get-tuple-element.15) | copy-start | bytes 3145732
  136.0 1.5 copy-start.23
  138.9 5.3 %copy-start.13 = (bf16[4,8,64,256]{3,2,1,0:T(8,128)(2,1)S(1)}, bf16[4,8,64,256]{3,2,1,0:T(8,128)(2,1)}, u32[]{:S(2)}) copy-start(bf16[4,8,64,256]{3,2,1,0:T(8,128)(2,1)} %get-tuple-element.18) | copy-start | bytes 3145732
  142.0 3.6 %copy-start.15 = (bf16[4,8,64,256]{3,2,1,0:T(8,128)(2,1)S(1)}, bf16[4,8,64,256]{3,2,1,0:T(8,128)(2,1)}, u32[]{:S(2)}) copy-start(bf16[4,8,64,256]{3,2,1,0:T(8,128)(2,1)} %get-tuple-element.13) | copy-start | bytes 3145732
  144.2 10.5 %collective-permute-start.8 = (bf16[8,12,16,256]{3,2,0,1:T(8,128)(2,1)}, bf16[8,12,16,256]{3,2,0,1:T(8,128)(2,1)}, u32[]{:S(2)}, u32[]{:S(2)}) collective-permute-start(bf16[8,12,16,256]{3,2,0,1:T(8,128)(2,1)} %copy.70), channel_id=1, source_target_pairs={{0,4},{4,0},{1,5},{5,1},{2,6},{6,2},{3,7},{7,3},{8,12},{12,8},{9,1... | collective-permute-start | bytes 2359304 | tf_op jit(solution)/shard_map/ppermute | solution.py:31
  145.6 1.5 copy-start.14
